TPU v7x, 32 devices: a whole 2x2x4 slice. The times are simulated.
32 devices in a mesh: ens: 2 (over x), lon: 16 (over z, y, core).
Axes of the slice: x: 2, y: 2, z: 4, core: 2. Of those that a mesh axis runs over, the one named last changes fastest.
Arguments:
- tracers: float32 [720, 32, 8, 128], P('lon', 'ens'), parts along dimension 1, may hold values from -6 to 6
- zonal_flux: float32 [64, 720, 128], P('ens', 'lon'), parts along dimension 0, may hold values from -0.3 to 0.3
- merid_flux: float32 [64, 720, 128], P('ens', 'lon'), parts along dimension 0, may hold values from -0.3 to 0.3
- kappa: float32 [128], replicated, may hold values from 0.1 to 100000
- levels: int32 [8], replicated, may hold values from 0 to 31
- groups: int32 [16], replicated, may hold values from 0 to 3
- emissions: float32 [4, 720, 128], P(None, 'lon'), may hold values from -4 to 8
- limiter: int32 [720, 128], P('lon'), may hold values 0 or 1
Outputs:
- updated: float32 [720, 32, 8, 128], P('lon', 'ens'), parts along dimension 1
There are 2 independent parts, one for each index of `ens`. A program takes and returns all parts, laid end to end along the dimension named above; an argument that names none is the same for every part. Nothing has to cross between parts.
Inputs may be any that keep to these rules, and one draw needn't show every extreme that they name: Slab levels may repeat and need not be ordered.
All inputs are finite; a program needn't handle non-finite values. No bound on the sum of `limiter` on one device may be relied on, other than what follows from the above.
Results may differ from a plain program's by a relative error of at most 0.0012.
Values sent between devices are 32-bit elements; how exact they have to be, the bound alone decides.
A program may use at most 128 MiB of HBM per device.

v0:
```python
import functools

import jax
import jax.numpy as jnp
from jax import lax
from jax.experimental import pallas as pl
from jax.experimental.pallas import tpu as pltpu
from jax.sharding import PartitionSpec as P

MESH = pl.DeviceIdType.MESH


def row(ref, index):
    return jnp.broadcast_to(ref[pl.ds(index, 1), :], (8, ref.shape[-1]))


def factor_units(n, kappa, coefs, back_s):
    half = kappa * 0.5

    def coef(d, c):
        return jnp.broadcast_to(coefs[d, pl.ds(c, 1), :], (8, kappa.shape[-1]))

    delta, z_prev = 1.0, 0.0
    ratios, zs = [], []
    for d in range(n):
        e = (d + 1) % n
        west = coef(e, 2)
        upper = west * 0.25 - half
        before = coef(d, 0)
        after = -upper * coef(e, 3)
        total = coef(d, 1) + west * 0.5 - upper * coef(e, 4)
        back_s[0, d] = upper
        if d < n - 1:
            num = total - before * delta
            inv = 1.0 / (num - after)
            delta = num * inv
            z_prev = total * inv - before * inv * z_prev
            back_s[1, d] = before * inv
            back_s[2, d] = inv
            ratio = after * inv
            back_s[3, d] = ratio
            ratios.append(ratio)
            zs.append(z_prev)
    for d in range(n - 3, -1, -1):
        zs[d] = zs[d] - ratios[d] * zs[d + 1]
    bottom = total - before * zs[n - 2] - after * zs[0]
    back_s[1, n - 1] = before
    back_s[2, n - 1] = 1.0 / bottom
    back_s[3, n - 1] = after
    for d in range(n - 1):
        back_s[4, d] = 1.0 - zs[d]


def solve_unit(n, back_s, gathered, solved):
    y_prev = 0.0
    ys = []
    for d in range(n):
        e = (d + 1) % n
        right = gathered[d, pl.ds(0, 8), :] - back_s[0, d] * gathered[e, pl.ds(8, 8), :]
        if d < n - 1:
            y_prev = right * back_s[2, d] - back_s[1, d] * y_prev
            ys.append(y_prev)
    for d in range(n - 3, -1, -1):
        ys[d] = ys[d] - back_s[3, d] * ys[d + 1]
    end = n - 1
    x_end = (right - back_s[1, end] * ys[end - 1] - back_s[3, end] * ys[0]) * back_s[2, end]
    solved[pl.ds(0, 8), :] = x_end
    solved[pl.ds(8 * n, 8), :] = x_end
    for d in range(n - 1):
        solved[pl.ds(8 * (d + 1), 8), :] = ys[d] + back_s[4, d] * x_end


def step_kernel(
    n,
    units,
    levels,
    groups,
    tracers_hbm,
    zonal_hbm,
    merid_hbm,
    kappa_ref,
    emissions_hbm,
    limiter_hbm,
    plain,
    w_ref,
    v_ref,
    out,
    tracers,
    zonal,
    merid,
    emissions,
    limiter,
    inv_s,
    low_s,
    ratio_s,
    g_s,
    p_s,
    q_s,
    c_s,
    c_message,
    message,
    coefs,
    gathered,
    back_s,
    solved,
    back,
    sem,
    s0,
    r0,
    s1,
    r1,
    s2,
    r2,
):
    cells, count, lev, lat = tracers.shape
    parts = count // 8
    last = cells - 1
    me = lax.axis_index("lon")
    ens = lax.axis_index("ens")
    every = n == units

    copies = [
        pltpu.make_async_copy(source, target, sem.at[at])
        for at, (source, target) in enumerate(
            (
                (zonal_hbm, zonal),
                (merid_hbm, merid),
                (emissions_hbm, emissions),
                (limiter_hbm, limiter),
                (tracers_hbm, tracers),
            )
        )
    ]
    for copy in copies:
        copy.start()
    barrier = pltpu.get_barrier_semaphore()

    def peer_of(step):
        return lax.rem(me + step, n)

    def source_of(step):
        return lax.rem(me + n - step, n)

    def when(condition):
        if every:
            return lambda f: f()
        return pl.when(condition)

    for step in range(1, n):
        pl.semaphore_signal(barrier, inc=1, device_id=(ens, peer_of(step)), device_id_type=MESH)

    def remote(source, target, send, recv, step):
        return pltpu.make_async_remote_copy(
            src_ref=source,
            dst_ref=target,
            send_sem=send.at[step],
            recv_sem=recv.at[step],
            device_id=(ens, peer_of(step)),
            device_id_type=MESH,
        )

    def early(step):
        return remote(c_message.at[peer_of(step)], coefs.at[me], s0, r0, step)

    def there(step):
        return remote(message.at[peer_of(step)], gathered.at[me], s1, r1, step)

    def home(step):
        return remote(
            solved.at[pl.ds(8 * peer_of(step), 16), :],
            back.at[pl.ds(16 * me, 16), :],
            s2,
            r2,
            step,
        )

    kappa = row(kappa_ref, 0)
    half = kappa * 0.5
    level = [levels[k] for k in range(lev)]
    group = [groups[t] for t in range(count)]
    lane = lax.broadcasted_iota(jnp.int32, (lev, lat), 1)
    sublane = lax.broadcasted_iota(jnp.int32, (lev, lat), 0)

    def at_cell(ref, i):
        value = jnp.broadcast_to(ref[i, pl.ds(level[0], 1), :], (lev, lat))
        for k in range(1, lev):
            other = jnp.broadcast_to(ref[i, pl.ds(level[k], 1), :], (lev, lat))
            value = jnp.where(sublane == k, other, value)
        return value

    def factor(i, carry):
        west, delta, w_prev, z_prev, g_here = carry
        east = at_cell(zonal, i + 1)
        lower = -(west * 0.25 + half)
        upper = east * 0.25 - half
        total = 1.0 + (east - west) * 0.5
        num = total - lower * delta
        inv = 1.0 / (num - upper)
        delta = num * inv
        low = lower * inv
        ratio = upper * inv
        w_here = -low * w_prev
        z_here = total * inv - low * z_prev
        inv_s[i] = inv
        low_s[i] = low
        ratio_s[i] = ratio
        g_s[i] = g_here
        w_ref[i] = w_here
        v_ref[i] = z_here
        return east, delta, w_here, z_here, -ratio * g_here

    copies[0].wait()
    west0 = at_cell(zonal, 0)
    ones = jnp.ones_like(west0)
    zeros = jnp.zeros_like(west0)
    west_last, _, w_last, z_last, _ = lax.fori_loop(
        0, last, factor, (west0, ones, -ones, zeros, ones), unroll=4
    )
    lower_last = -(west_last * 0.25 + half)

    def spikes(step, carry):
        i = last - 1 - step
        w_next, v_next, z_next = carry
        ratio = ratio_s[i]
        z_here = v_ref[i] - ratio * z_next
        w_here = w_ref[i] - ratio * w_next
        v_here = -ratio * v_next
        w_ref[i] = w_here
        v_ref[i] = v_here
        return w_here, v_here, z_here

    _, v_first, z_first = lax.fori_loop(0, last, spikes, (zeros, -ones, zeros), unroll=4)
    w_ref[last] = zeros
    v_ref[last] = -ones

    columns = (
        -lower_last * w_last,
        1.0 - west_last * 0.5 - lower_last * z_last,
        west0,
        v_first,
        z_first,
        zeros,
        zeros,
        zeros,
    )
    for at, column in enumerate(columns):
        c_s[pl.ds(8 * at, 8), :] = column
    for k in range(lev):
        for h in range(parts):
            c_message[k * parts + h] = c_s[pl.ds(k, 8, stride=8), :]
    for copy in copies[1:]:
        copy.wait()

    def rights(i):
        face = jnp.where(lane > 0, at_cell(merid, i), 0.0)
        upwind = jnp.where(face > 0, 1.0, 0.0)
        share = jnp.where(row(limiter, i) == 1, upwind, 0.5)
        south = face * share
        north = face * (1.0 - share)
        here = 2.0 + north - pltpu.roll(south, lat - 1, 1)
        after = -pltpu.roll(north, lat - 1, 1)
        result = []
        for t in range(count):
            value = tracers[i, t]
            source = jnp.broadcast_to(emissions[i, pl.ds(group[t], 1), :], (lev, lat))
            result.append(
                south * pltpu.roll(value, 1, 1)
                + here * value
                + (after * pltpu.roll(value, lat - 1, 1) + source)
            )
        return result

    def forward(i, carry):
        inv = inv_s[i]
        low = low_s[i]
        weight = g_s[i]
        values, firsts = [], []
        for t, right in enumerate(rights(i)):
            value = right * inv - low * carry[0][t]
            plain[i, t] = value
            values.append(value)
            firsts.append(carry[1][t] + weight * value)
        return tuple(values), tuple(firsts)

    ends, firsts = lax.fori_loop(
        0, last, forward, ((zeros,) * count, (zeros,) * count), unroll=2
    )
    for t, right in enumerate(rights(last)):
        p_s[pl.ds(t * lev, lev), :] = right - lower_last * ends[t]
        q_s[pl.ds(t * lev, lev), :] = firsts[t]
    for k in range(lev):
        for h in range(parts):
            unit = k * parts + h
            rows = pl.ds(h * 8 * lev + k, 8, stride=lev)
            message[unit, pl.ds(0, 8), :] = p_s[rows, :]
            message[unit, pl.ds(8, 8), :] = q_s[rows, :]
    pl.semaphore_wait(barrier, n - 1)
    for step in range(1, n):

        @when(peer_of(step) < units)
        def _():
            early(step).start()

    for step in range(1, n):

        @when(peer_of(step) < units)
        def _():
            there(step).start()

    @when(me < units)
    def _():
        coefs[me] = c_message[me]
        gathered[me] = message[me]
        for step in range(1, n):
            early(step).wait_recv()
        factor_units(n, kappa, coefs, back_s)

    def backward(step, carry):
        i = last - 1 - step
        ratio = ratio_s[i]
        result = []
        for t in range(count):
            value = plain[i, t] - ratio * carry[t]
            plain[i, t] = value - tracers[i, t]
            result.append(value)
        return tuple(result)

    lax.fori_loop(0, last, backward, (zeros,) * count, unroll=4)
    for t in range(count):
        plain[last, t] = -tracers[last, t]

    @when(me < units)
    def _():
        for step in range(1, n):
            there(step).wait_recv()
        solve_unit(n, back_s, gathered, solved)
        for step in range(1, n):
            home(step).start()
        back[pl.ds(16 * me, 16), :] = solved[pl.ds(8 * me, 16), :]

    for step in range(1, n):

        @when(peer_of(step) < units)
        def _():
            early(step).wait_send()
            there(step).wait_send()

    for step in range(1, n):

        @when(source_of(step) < units)
        def _():
            home(step).wait_recv()

    for j in range(2):
        for h in range(parts):
            for t in range(8):
                out[j, h * 8 + t] = back[pl.ds((h * 2 + j) * 8 + t, lev, stride=16 * parts), :]

    @when(me < units)
    def _():
        for step in range(1, n):
            home(step).wait_send()


def combine_kernel(cuts, plain, w_s, v_s, edges, out_hbm, buffer, done):
    count = buffer.shape[1]
    parts = [pl.ds(low, high - low) for low, high in zip(cuts[:-1], cuts[1:])]
    outs = [
        pltpu.make_async_copy(buffer.at[part], out_hbm.at[part], done.at[at])
        for at, part in enumerate(parts)
    ]

    def at_cell(i, carry):
        w_here, v_here = w_s[i], v_s[i]
        for t in range(count):
            buffer[i, t] = plain[i, t] - (w_here * edges[0, t] + v_here * edges[1, t])
        return carry

    for at in range(len(parts)):
        lax.fori_loop(cuts[at], cuts[at + 1], at_cell, 0, unroll=3)
        outs[at].start()
    for copy in outs:
        copy.wait()


def on_device(tracers, zonal_flux, merid_flux, kappa, levels, groups, emissions, limiter):
    n = lax.axis_size("lon")
    cells, count, lev, lat = tracers.shape
    units = lev * (count // 8)
    assert lev == 8 and count % 8 == 0 and n >= units
    f32 = jnp.float32
    hbm = pl.BlockSpec(memory_space=pl.ANY)
    vmem = pl.BlockSpec(memory_space=pltpu.VMEM)
    smem = pl.BlockSpec(memory_space=pltpu.SMEM)
    kappa = kappa.reshape(1, lat)
    zonal_flux, merid_flux, emissions = (
        jnp.swapaxes(value, 0, 1) for value in (zonal_flux, merid_flux, emissions)
    )
    column = (cells, lev, lat)
    levels, groups, tracers, zonal_flux, merid_flux, kappa, emissions, limiter = (
        pltpu.with_memory_space_constraint(value, pltpu.HBM)
        for value in (
            levels,
            groups,
            tracers,
            zonal_flux,
            merid_flux,
            kappa,
            emissions,
            limiter,
        )
    )
    plain, w_spike, v_spike, edges = pl.pallas_call(
        functools.partial(step_kernel, n, units),
        out_shape=(
            pltpu.VMEM(tracers.shape, f32),
            pltpu.VMEM(column, f32),
            pltpu.VMEM(column, f32),
            pltpu.VMEM((2, count, lev, lat), f32),
        ),
        in_specs=[smem, smem, hbm, hbm, hbm, vmem, hbm, hbm],
        out_specs=(vmem,) * 4,
        scratch_shapes=[
            pltpu.VMEM(tracers.shape, f32),
            pltpu.VMEM(zonal_flux.shape, f32),
            pltpu.VMEM(merid_flux.shape, f32),
            pltpu.VMEM(emissions.shape, f32),
            pltpu.VMEM(limiter.shape, jnp.int32),
        ]
        + [pltpu.VMEM(column, f32)] * 4
        + [
            pltpu.VMEM((count * lev, lat), f32),
            pltpu.VMEM((count * lev, lat), f32),
            pltpu.VMEM((64, lat), f32),
            pltpu.VMEM((units, 8, lat), f32),
            pltpu.VMEM((units, 16, lat), f32),
            pltpu.VMEM((n, 8, lat), f32),
            pltpu.VMEM((n, 16, lat), f32),
            pltpu.VMEM((5, n, 8, lat), f32),
            pltpu.VMEM((8 * (n + 1), lat), f32),
            pltpu.VMEM((units * 16, lat), f32),
            pltpu.SemaphoreType.DMA((5,)),
        ]
        + [pltpu.SemaphoreType.DMA((n,))] * 6,
        compiler_params=pltpu.CompilerParams(
            collective_id=0, has_side_effects=True, vmem_limit_bytes=32 << 20
        ),
        name="transport_step",
    )(levels, groups, tracers, zonal_flux, merid_flux, kappa, emissions, limiter)
    pieces = 5
    cuts = [cells * at // pieces for at in range(pieces + 1)]
    return pl.pallas_call(
        functools.partial(combine_kernel, cuts),
        out_shape=jax.ShapeDtypeStruct(tracers.shape, f32),
        in_specs=[vmem] * 4,
        out_specs=hbm,
        scratch_shapes=[
            pltpu.VMEM(tracers.shape, f32),
            pltpu.SemaphoreType.DMA((pieces,)),
        ],
        compiler_params=pltpu.CompilerParams(vmem_limit_bytes=32 << 20),
        name="combine",
    )(plain, w_spike, v_spike, edges)


def solution(mesh):
    placed = (
        P("lon", "ens", None, None),
        P("ens", "lon", None),
        P("ens", "lon", None),
        P(),
        P(),
        P(),
        P(None, "lon", None),
        P("lon", None),
    )
    return jax.shard_map(
        on_device,
        mesh=mesh,
        in_specs=placed,
        out_specs=P("lon", "ens", None, None),
        check_vma=False,
    )
```

profile of v0, /device:TPU:0, one launch (start us, length us, event | category | flops | bytes accessed | tf_op | source)
XLA Modules:
  0.0 22.2 jit_solution(13151628269130825717)
XLA Ops:
  0.0 20.5 %transport_step.1 = (f32[45,16,8,128]{3,2,1,0:T(8,128)S(1)}, f32[45,8,128]{2,1,0:T(8,128)S(1)}, f32[45,8,128]{2,1,0:T(8,128)S(1)}, f32[2,16,8,128]{3,2,1,0:T(8,128)S(1)}) custom-call(s32[8]{0:T(128)} %levels.1, s32[16]{0:T(128)} %groups.1, f32[45,16,8,128]{3,2,1,0:T(8,128)} %tracers_hbm.1, f32[45,32,128]{2,1,0:T(8,128)} %bitcast.4, f32[45,32,128]{2,1,0:T(8,128)} %bitcast.5, ...), custom_call_target="tpu_custom_call" | custom-call | tf_op jit(solution)/shard_map/transport_step/pallas_call | solution.py:413
  20.5 1.7 %combine.1 = f32[45,16,8,128]{3,2,1,0:T(8,128)} custom-call(f32[45,16,8,128]{3,2,1,0:T(8,128)S(1)} %get-tuple-element.9.plain, f32[45,8,128]{2,1,0:T(8,128)S(1)} %get-tuple-element.10.w_s, f32[45,8,128]{2,1,0:T(8,128)S(1)} %get-tuple-element.11.v_s, f32[2,16,8,128]{3,2,1,0:T(8,128)S(1)} %get-tuple-element.12.edges), custom_call_target="tpu_custom_call" | custom-call | tf_op jit(solution)/shard_map/combine/pallas_call | solution.py:452
where the time goes:
time: 22.4 us; the launch traced here: 22.2 us
  Pallas kernels  22.2 us (99%)
    pallas_call x1, Pallas kernels, on_device(): pl.pallas_call(functools.partial(step_kernel, n, units), out_shape=(pltpu...  20.5 us
    pallas_call x1, Pallas kernels, on_device(): pl.pallas_call(functools.partial(combine_kernel, cuts), out_shape=jax.Sha...  1.74 us

commit v1 on v0

v1 whole, which is shorter than its diff:
```python
import functools

import jax
import jax.numpy as jnp
from jax import lax
from jax.experimental import pallas as pl
from jax.experimental.pallas import tpu as pltpu
from jax.sharding import PartitionSpec as P

MESH = pl.DeviceIdType.MESH


def row(ref, index):
    return jnp.broadcast_to(ref[pl.ds(index, 1), :], (8, ref.shape[-1]))


def factor_levels(n, kappa, coefs, back_s):
    half = kappa * 0.5

    def coef(d, c):
        return jnp.broadcast_to(coefs[d, pl.ds(c, 1), :], (8, kappa.shape[-1]))

    delta, z_prev = 1.0, 0.0
    ratios, zs = [], []
    for d in range(n):
        e = (d + 1) % n
        west = coef(e, 2)
        upper = west * 0.25 - half
        before = coef(d, 0)
        after = -upper * coef(e, 3)
        total = coef(d, 1) + west * 0.5 - upper * coef(e, 4)
        back_s[0, d] = upper
        if d < n - 1:
            num = total - before * delta
            inv = 1.0 / (num - after)
            delta = num * inv
            z_prev = total * inv - before * inv * z_prev
            back_s[1, d] = before * inv
            back_s[2, d] = inv
            ratio = after * inv
            back_s[3, d] = ratio
            ratios.append(ratio)
            zs.append(z_prev)
    for d in range(n - 3, -1, -1):
        zs[d] = zs[d] - ratios[d] * zs[d + 1]
    bottom = total - before * zs[n - 2] - after * zs[0]
    back_s[1, n - 1] = before
    back_s[2, n - 1] = 1.0 / bottom
    back_s[3, n - 1] = after
    for d in range(n - 1):
        back_s[4, d] = 1.0 - zs[d]


def solve_level(n, h, back_s, gathered, solved):
    y_prev = 0.0
    ys = []
    for d in range(n):
        e = (d + 1) % n
        right = gathered[h, d, pl.ds(0, 8), :] - back_s[0, d] * gathered[h, e, pl.ds(8, 8), :]
        if d < n - 1:
            y_prev = right * back_s[2, d] - back_s[1, d] * y_prev
            ys.append(y_prev)
    for d in range(n - 3, -1, -1):
        ys[d] = ys[d] - back_s[3, d] * ys[d + 1]
    end = n - 1
    x_end = (right - back_s[1, end] * ys[end - 1] - back_s[3, end] * ys[0]) * back_s[2, end]
    solved[h, pl.ds(0, 8), :] = x_end
    solved[h, pl.ds(8 * n, 8), :] = x_end
    for d in range(n - 1):
        solved[h, pl.ds(8 * (d + 1), 8), :] = ys[d] + back_s[4, d] * x_end


def step_kernel(
    n,
    first_owner,
    levels_hbm,
    groups_hbm,
    tracers_hbm,
    zonal_hbm,
    merid_hbm,
    kappa_hbm,
    emissions_hbm,
    limiter_hbm,
    plain,
    w_ref,
    v_ref,
    out,
    levels,
    groups,
    kappa_ref,
    tracers,
    zonal,
    merid,
    emissions,
    limiter,
    low_s,
    ratio_s,
    g_s,
    south_s,
    here_s,
    after_s,
    source_s,
    p_s,
    q_s,
    c_s,
    c_message,
    message,
    coefs,
    gathered,
    back_s,
    solved,
    back,
    sem,
    s0,
    r0,
    s1,
    r1,
    s2,
    r2,
):
    cells, count, lev, lat = tracers.shape
    kinds = emissions.shape[1]
    parts = count // 8
    last = cells - 1
    me = lax.axis_index("lon")
    ens = lax.axis_index("ens")
    is_owner = jnp.logical_and(me >= first_owner, me < first_owner + lev)
    mine = me - first_owner

    halves = [pl.ds(8 * h, 8) for h in range(parts)]
    copies = [
        pltpu.make_async_copy(source, target, sem.at[at])
        for at, (source, target) in enumerate(
            [
                (levels_hbm, levels),
                (kappa_hbm, kappa_ref),
                (zonal_hbm, zonal),
                (merid_hbm, merid),
                (limiter_hbm, limiter),
                (groups_hbm, groups),
                (emissions_hbm, emissions),
            ]
            + [(tracers_hbm.at[:, half], tracers.at[:, half]) for half in halves]
        )
    ]
    for copy in copies[:4]:
        copy.start()
    barrier = pltpu.get_barrier_semaphore()
    for k in range(lev):

        @pl.when(first_owner + k != me)
        def _():
            pl.semaphore_signal(
                barrier, inc=1, device_id=(ens, first_owner + k), device_id_type=MESH
            )

    @pl.when(is_owner)
    def _():
        for d in range(n):
            if d < first_owner or d >= first_owner + lev:
                pl.semaphore_signal(barrier, inc=1, device_id=(ens, d), device_id_type=MESH)

    for copy in copies[4:]:
        copy.start()

    def remote(source, target, send, recv, device):
        return pltpu.make_async_remote_copy(
            src_ref=source,
            dst_ref=target,
            send_sem=send,
            recv_sem=recv,
            device_id=(ens, device),
            device_id_type=MESH,
        )

    def early(k, sender):
        return remote(
            c_message.at[k], coefs.at[sender], s0.at[k], r0.at[sender], first_owner + k
        )

    def there(h, k, sender):
        return remote(
            message.at[h, k],
            gathered.at[h, sender],
            s1.at[h, k],
            r1.at[h, sender],
            first_owner + k,
        )

    def home(h, k, device):
        return remote(
            solved.at[h, pl.ds(8 * device, 16), :],
            back.at[h, pl.ds(16 * k, 16), :],
            s2.at[h, device],
            r2.at[h, k],
            device,
        )

    for copy in copies[:3]:
        copy.wait()
    kappa = row(kappa_ref, 0)
    half = kappa * 0.5
    level = [levels[k] for k in range(lev)]
    lane = lax.broadcasted_iota(jnp.int32, (lev, lat), 1)
    sublane = lax.broadcasted_iota(jnp.int32, (lev, lat), 0)

    def at_cell(ref, i):
        value = jnp.broadcast_to(ref[i, pl.ds(level[0], 1), :], (lev, lat))
        for k in range(1, lev):
            other = jnp.broadcast_to(ref[i, pl.ds(level[k], 1), :], (lev, lat))
            value = jnp.where(sublane == k, other, value)
        return value

    def prepare(i, inv):
        face = jnp.where(lane > 0, at_cell(merid, i), 0.0)
        upwind = jnp.where(face > 0, 1.0, 0.0)
        share = jnp.where(row(limiter, i) == 1, upwind, 0.5)
        south = face * share
        north = face - south
        south_s[i] = south * inv
        here_s[i] = (2.0 + north - pltpu.roll(south, lat - 1, 1)) * inv
        after_s[i] = pltpu.roll(north, lat - 1, 1) * inv
        for g in range(kinds):
            value = jnp.broadcast_to(emissions[i, pl.ds(g, 1), :], (lev, lat))
            source_s[i * kinds + g] = value * inv

    def factor(i, carry):
        west, delta, w_prev, z_prev, g_here, z_first = carry
        east = at_cell(zonal, i + 1)
        lower = -(west * 0.25 + half)
        upper = east * 0.25 - half
        total = 1.0 + (east - west) * 0.5
        num = total - lower * delta
        inv = 1.0 / (num - upper)
        delta = num * inv
        low = lower * inv
        ratio = upper * inv
        w_here = -low * w_prev
        z_here = total * inv - low * z_prev
        low_s[i] = low
        ratio_s[i] = ratio
        g_s[i] = g_here
        w_ref[i] = w_here
        prepare(i, inv)
        return east, delta, w_here, z_here, -ratio * g_here, z_first + g_here * z_here

    for copy in copies[3:7]:
        copy.wait()
    group = [groups[t] for t in range(count)]
    west0 = at_cell(zonal, 0)
    ones = jnp.ones_like(west0)
    zeros = jnp.zeros_like(west0)
    west_last, _, w_last, z_last, g_end, z_first = lax.fori_loop(
        0, last, factor, (west0, ones, -ones, zeros, ones, zeros), unroll=4
    )
    prepare(last, ones)
    lower_last = -(west_last * 0.25 + half)

    columns = (
        -lower_last * w_last,
        1.0 - west_last * 0.5 - lower_last * z_last,
        west0,
        -g_end,
        z_first,
        zeros,
        zeros,
        zeros,
    )
    for at, column in enumerate(columns):
        c_s[pl.ds(8 * at, 8), :] = column
    for k in range(lev):
        c_message[k] = c_s[pl.ds(k, 8, stride=8), :]

    def shifted(i, h):
        values = [tracers[i, 8 * h + t] for t in range(8)]
        return (
            tuple(pltpu.roll(value, 1, 1) for value in values),
            tuple(pltpu.roll(value, lat - 1, 1) for value in values),
        )

    def rights(h, i, souths, norths):
        south, here, after = south_s[i], here_s[i], after_s[i]
        return [
            south * souths[t]
            + here * tracers[i, 8 * h + t]
            + (source_s[i * kinds + group[8 * h + t]] - after * norths[t])
            for t in range(8)
        ]

    def forward(h, i, carry):
        before, sums, souths, norths = carry
        low, weight = low_s[i], g_s[i]
        values, firsts = [], []
        for t, right in enumerate(rights(h, i, souths, norths)):
            value = right - low * before[t]
            plain[i, 8 * h + t] = value
            values.append(value)
            firsts.append(sums[t] + weight * value)
        return (tuple(values), tuple(firsts), *shifted(i + 1, h))

    def sweep(h):
        copies[7 + h].wait()
        nothing = (zeros,) * 8
        ends, firsts, souths, norths = lax.fori_loop(
            0, last, functools.partial(forward, h), (nothing, nothing, *shifted(0, h)), unroll=4
        )
        for t, right in enumerate(rights(h, last, souths, norths)):
            p_s[pl.ds(t * lev, lev), :] = right - lower_last * ends[t]
            q_s[pl.ds(t * lev, lev), :] = firsts[t]
        for k in range(lev):
            rows = pl.ds(k, 8, stride=lev)
            message[h, k, pl.ds(0, 8), :] = p_s[rows, :]
            message[h, k, pl.ds(8, 8), :] = q_s[rows, :]

    def send(copy_of):
        for k in range(lev):

            @pl.when(first_owner + k != me)
            def _():
                copy_of(k).start()

    for h in range(parts):
        sweep(h)
        if h == 0:

            @pl.when(is_owner)
            def _():
                pl.semaphore_wait(barrier, n - 1)

            @pl.when(jnp.logical_not(is_owner))
            def _():
                pl.semaphore_wait(barrier, lev)

            send(lambda k: early(k, me))
            for g in range(h):
                send(lambda k: there(g, k, me))
        if h >= 0:
            send(lambda k: there(h, k, me))

    @pl.when(is_owner)
    def _():
        coefs[me] = c_message[mine]
        for h in range(parts):
            gathered[h, me] = message[h, mine]

    def spikes(step, carry):
        i = last - 1 - step
        w_next, v_next = carry
        ratio = ratio_s[i]
        w_here = w_ref[i] - ratio * w_next
        v_here = -ratio * v_next
        w_ref[i] = w_here
        v_ref[i] = v_here
        return w_here, v_here

    lax.fori_loop(0, last, spikes, (zeros, -ones), unroll=4)
    w_ref[last] = zeros
    v_ref[last] = -ones

    def backward(step, carry):
        i = last - 1 - step
        ratio = ratio_s[i]
        result = []
        for t in range(count):
            value = plain[i, t] - ratio * carry[t]
            plain[i, t] = value - tracers[i, t]
            result.append(value)
        return tuple(result)

    lax.fori_loop(0, last, backward, (zeros,) * count, unroll=4)
    for t in range(count):
        plain[last, t] = -tracers[last, t]

    @pl.when(is_owner)
    def _():
        senders = [lax.rem(me + step, n) for step in range(1, n)]
        for d in senders:
            early(mine, d).wait_recv()
        factor_levels(n, kappa, coefs, back_s)
        for h in range(parts):
            for d in senders:
                there(h, mine, d).wait_recv()
            solve_level(n, h, back_s, gathered, solved)
            for d in senders:
                home(h, mine, d).start()
            back[h, pl.ds(16 * mine, 16), :] = solved[h, pl.ds(8 * me, 16), :]

    for h in range(parts):
        for k in range(lev):

            @pl.when(first_owner + k != me)
            def _():
                home(h, k, me).wait_recv()

        for j in range(2):
            for t in range(8):
                out[j, h * 8 + t] = back[h, pl.ds(j * 8 + t, lev, stride=16), :]

    for k in range(lev):

        @pl.when(first_owner + k != me)
        def _():
            early(k, me).wait_send()
            for h in range(parts):
                there(h, k, me).wait_send()

    @pl.when(is_owner)
    def _():
        for h in range(parts):
            for step in range(1, n):
                home(h, mine, lax.rem(me + step, n)).wait_send()


def combine_kernel(cuts, plain, w_s, v_s, edges, out_hbm, buffer, done):
    count = buffer.shape[1]
    parts = [pl.ds(low, high - low) for low, high in zip(cuts[:-1], cuts[1:])]
    outs = [
        pltpu.make_async_copy(buffer.at[part], out_hbm.at[part], done.at[at])
        for at, part in enumerate(parts)
    ]

    def at_cell(i, carry):
        w_here, v_here = w_s[i], v_s[i]
        for t in range(count):
            buffer[i, t] = plain[i, t] - (w_here * edges[0, t] + v_here * edges[1, t])
        return carry

    for at in range(len(parts)):
        lax.fori_loop(cuts[at], cuts[at + 1], at_cell, 0, unroll=3)
        outs[at].start()
    for copy in outs:
        copy.wait()


def on_device(tracers, zonal_flux, merid_flux, kappa, levels, groups, emissions, limiter):
    n = lax.axis_size("lon")
    cells, count, lev, lat = tracers.shape
    parts, kinds = count // 8, emissions.shape[0]
    first_owner = (n - lev) // 2
    assert lev == 8 and count % 8 == 0 and n >= lev
    f32 = jnp.float32
    hbm = pl.BlockSpec(memory_space=pl.ANY)
    vmem = pl.BlockSpec(memory_space=pltpu.VMEM)
    kappa = kappa.reshape(1, lat)
    zonal_flux, merid_flux, emissions = (
        jnp.swapaxes(value, 0, 1) for value in (zonal_flux, merid_flux, emissions)
    )
    column = (cells, lev, lat)
    levels, groups, tracers, zonal_flux, merid_flux, kappa, emissions, limiter = (
        pltpu.with_memory_space_constraint(value, pltpu.HBM)
        for value in (
            levels,
            groups,
            tracers,
            zonal_flux,
            merid_flux,
            kappa,
            emissions,
            limiter,
        )
    )
    plain, w_spike, v_spike, edges = pl.pallas_call(
        functools.partial(step_kernel, n, first_owner),
        out_shape=(
            pltpu.VMEM(tracers.shape, f32),
            pltpu.VMEM(column, f32),
            pltpu.VMEM(column, f32),
            pltpu.VMEM((2, count, lev, lat), f32),
        ),
        in_specs=[hbm] * 8,
        out_specs=(vmem,) * 4,
        scratch_shapes=[
            pltpu.SMEM(levels.shape, jnp.int32),
            pltpu.SMEM(groups.shape, jnp.int32),
            pltpu.VMEM(kappa.shape, f32),
            pltpu.VMEM(tracers.shape, f32),
            pltpu.VMEM(zonal_flux.shape, f32),
            pltpu.VMEM(merid_flux.shape, f32),
            pltpu.VMEM(emissions.shape, f32),
            pltpu.VMEM(limiter.shape, jnp.int32),
        ]
        + [pltpu.VMEM(column, f32)] * 6
        + [
            pltpu.VMEM((cells * kinds, lev, lat), f32),
            pltpu.VMEM((8 * lev, lat), f32),
            pltpu.VMEM((8 * lev, lat), f32),
            pltpu.VMEM((64, lat), f32),
            pltpu.VMEM((lev, 8, lat), f32),
            pltpu.VMEM((parts, lev, 16, lat), f32),
            pltpu.VMEM((n, 8, lat), f32),
            pltpu.VMEM((parts, n, 16, lat), f32),
            pltpu.VMEM((5, n, 8, lat), f32),
            pltpu.VMEM((parts, 8 * (n + 1), lat), f32),
            pltpu.VMEM((parts, 16 * lev, lat), f32),
            pltpu.SemaphoreType.DMA((7 + parts,)),
            pltpu.SemaphoreType.DMA((lev,)),
            pltpu.SemaphoreType.DMA((n,)),
            pltpu.SemaphoreType.DMA((parts, lev)),
            pltpu.SemaphoreType.DMA((parts, n)),
            pltpu.SemaphoreType.DMA((parts, n)),
            pltpu.SemaphoreType.DMA((parts, lev)),
        ],
        compiler_params=pltpu.CompilerParams(
            collective_id=0, has_side_effects=True, vmem_limit_bytes=32 << 20
        ),
        name="transport_step",
    )(levels, groups, tracers, zonal_flux, merid_flux, kappa, emissions, limiter)
    pieces = 5
    cuts = [cells * at // pieces for at in range(pieces + 1)]
    return pl.pallas_call(
        functools.partial(combine_kernel, cuts),
        out_shape=jax.ShapeDtypeStruct(tracers.shape, f32),
        in_specs=[vmem] * 4,
        out_specs=hbm,
        scratch_shapes=[
            pltpu.VMEM(tracers.shape, f32),
            pltpu.SemaphoreType.DMA((pieces,)),
        ],
        compiler_params=pltpu.CompilerParams(vmem_limit_bytes=32 << 20),
        name="combine",
    )(plain, w_spike, v_spike, edges)


def solution(mesh):
    placed = (
        P("lon", "ens", None, None),
        P("ens", "lon", None),
        P("ens", "lon", None),
        P(),
        P(),
        P(),
        P(None, "lon", None),
        P("lon", None),
    )
    return jax.shard_map(
        on_device,
        mesh=mesh,
        in_specs=placed,
        out_specs=P("lon", "ens", None, None),
        check_vma=False,
    )
```

time: 22.4 us -> 20.2 us (0.902)
  Pallas kernels: 22.2 us -> 20 us
    pallas_call x1, Pallas kernels: 20.5 us -> 18.3 us  [on_device(): pl.pallas_call(functools.partial(step_kernel, n, first_owner), out_shape=...]
where the time goes in v1:
time: 20.2 us; the launch traced here: 20 us
  Pallas kernels  20 us (99%)
    pallas_call x1, Pallas kernels, on_device(): pl.pallas_call(functools.partial(step_kernel, n, first_owner), out_shape=...  18.3 us
    pallas_call x1, Pallas kernels, on_device(): pl.pallas_call(functools.partial(combine_kernel, cuts), out_shape=jax.Sha...  1.74 us

profile of v1, /device:TPU:0, one launch (start us, length us, event | category | flops | bytes accessed | tf_op | source)
XLA Modules:
  0.0 20.0 jit_solution(7600357444713654892)
XLA Ops:
  0.0 18.3 %transport_step.1 = (f32[45,16,8,128]{3,2,1,0:T(8,128)S(1)}, f32[45,8,128]{2,1,0:T(8,128)S(1)}, f32[45,8,128]{2,1,0:T(8,128)S(1)}, f32[2,16,8,128]{3,2,1,0:T(8,128)S(1)}) custom-call(s32[8]{0:T(128)} %levels_hbm.1, s32[16]{0:T(128)} %groups_hbm.1, f32[45,16,8,128]{3,2,1,0:T(8,128)} %tracers_hbm.1, f32[45,32,128]{2,1,0:T(8,128)} %bitcast.4, ...), custom_call_target="tpu_custom_call" | custom-call | tf_op jit(solution)/shard_map/transport_step/pallas_call | solution.py:462
  18.3 1.7 %combine.1 = f32[45,16,8,128]{3,2,1,0:T(8,128)} custom-call(f32[45,16,8,128]{3,2,1,0:T(8,128)S(1)} %get-tuple-element.9.plain, f32[45,8,128]{2,1,0:T(8,128)S(1)} %get-tuple-element.10.w_s, f32[45,8,128]{2,1,0:T(8,128)S(1)} %get-tuple-element.11.v_s, f32[2,16,8,128]{3,2,1,0:T(8,128)S(1)} %get-tuple-element.12.edges), custom_call_target="tpu_custom_call" | custom-call | tf_op jit(solution)/shard_map/combine/pallas_call | solution.py:510

commit v2 on v1

--- a/solution.py
+++ b/solution.py
@@ -111,12 +111,7 @@
     solved,
     back,
     sem,
-    s0,
-    r0,
-    s1,
-    r1,
-    s2,
-    r2,
+    wave,
 ):
     cells, count, lev, lat = tracers.shape
     kinds = emissions.shape[1]
@@ -146,19 +141,19 @@
     for copy in copies[:4]:
         copy.start()
     barrier = pltpu.get_barrier_semaphore()
-    for k in range(lev):
-
-        @pl.when(first_owner + k != me)
-        def _():
-            pl.semaphore_signal(
-                barrier, inc=1, device_id=(ens, first_owner + k), device_id_type=MESH
-            )
+
+    def greet(device):
+        pl.semaphore_signal(barrier, inc=1, device_id=(ens, device), device_id_type=MESH)
 
     @pl.when(is_owner)
     def _():
-        for d in range(n):
-            if d < first_owner or d >= first_owner + lev:
-                pl.semaphore_signal(barrier, inc=1, device_id=(ens, d), device_id_type=MESH)
+        for step in range(1, n):
+            greet(lax.rem(me + step, n))
+
+    @pl.when(jnp.logical_not(is_owner))
+    def _():
+        for k in range(lev):
+            greet(first_owner + k)
 
     for copy in copies[4:]:
         copy.start()
@@ -175,15 +170,15 @@
 
     def early(k, sender):
         return remote(
-            c_message.at[k], coefs.at[sender], s0.at[k], r0.at[sender], first_owner + k
+            c_message.at[k], coefs.at[sender], wave.at[0], wave.at[1], first_owner + k
         )
 
     def there(h, k, sender):
         return remote(
             message.at[h, k],
             gathered.at[h, sender],
-            s1.at[h, k],
-            r1.at[h, sender],
+            wave.at[2 + h],
+            wave.at[2 + parts + h],
             first_owner + k,
         )
 
@@ -191,8 +186,8 @@
         return remote(
             solved.at[h, pl.ds(8 * device, 16), :],
             back.at[h, pl.ds(16 * k, 16), :],
-            s2.at[h, device],
-            r2.at[h, k],
+            wave.at[2 + 2 * parts + h],
+            wave.at[2 + 3 * parts + h],
             device,
         )
 
@@ -251,7 +246,7 @@
     ones = jnp.ones_like(west0)
     zeros = jnp.zeros_like(west0)
     west_last, _, w_last, z_last, g_end, z_first = lax.fori_loop(
-        0, last, factor, (west0, ones, -ones, zeros, ones, zeros), unroll=4
+        0, last, factor, (west0, ones, -ones, zeros, ones, zeros), unroll=11
     )
     prepare(last, ones)
     lower_last = -(west_last * 0.25 + half)
@@ -302,7 +297,7 @@
         copies[7 + h].wait()
         nothing = (zeros,) * 8
         ends, firsts, souths, norths = lax.fori_loop(
-            0, last, functools.partial(forward, h), (nothing, nothing, *shifted(0, h)), unroll=4
+            0, last, functools.partial(forward, h), (nothing, nothing, *shifted(0, h)), unroll=22
         )
         for t, right in enumerate(rights(h, last, souths, norths)):
             p_s[pl.ds(t * lev, lev), :] = right - lower_last * ends[t]
@@ -313,11 +308,18 @@
             message[h, k, pl.ds(8, 8), :] = q_s[rows, :]
 
     def send(copy_of):
-        for k in range(lev):
-
-            @pl.when(first_owner + k != me)
-            def _():
+        @pl.when(is_owner)
+        def _():
+            for step in range(1, lev):
+                copy_of(lax.rem(mine + step, lev)).start()
+
+        @pl.when(jnp.logical_not(is_owner))
+        def _():
+            for k in range(lev):
                 copy_of(k).start()
+
+    def settle(block, at):
+        pltpu.make_async_copy(block, block, wave.at[at]).wait()
 
     for h in range(parts):
         sweep(h)
@@ -373,42 +375,47 @@
 
     @pl.when(is_owner)
     def _():
-        senders = [lax.rem(me + step, n) for step in range(1, n)]
-        for d in senders:
-            early(mine, d).wait_recv()
+        others = pl.ds(0, n - 1)
+        settle(coefs.at[others], 1)
         factor_levels(n, kappa, coefs, back_s)
         for h in range(parts):
-            for d in senders:
-                there(h, mine, d).wait_recv()
+            settle(gathered.at[h, others], 2 + parts + h)
             solve_level(n, h, back_s, gathered, solved)
-            for d in senders:
-                home(h, mine, d).start()
+            for step in range(n - 1):
+                home(h, mine, step + jnp.where(step < me, 0, 1)).start()
             back[h, pl.ds(16 * mine, 16), :] = solved[h, pl.ds(8 * me, 16), :]
 
+    def finish(h, owners):
+        settle(back.at[h, pl.ds(0, 16 * owners)], 2 + 3 * parts + h)
+
     for h in range(parts):
-        for k in range(lev):
-
-            @pl.when(first_owner + k != me)
-            def _():
-                home(h, k, me).wait_recv()
+
+        @pl.when(is_owner)
+        def _():
+            finish(h, lev - 1)
+
+        @pl.when(jnp.logical_not(is_owner))
+        def _():
+            finish(h, lev)
 
         for j in range(2):
             for t in range(8):
                 out[j, h * 8 + t] = back[h, pl.ds(j * 8 + t, lev, stride=16), :]
 
-    for k in range(lev):
-
-        @pl.when(first_owner + k != me)
-        def _():
-            early(k, me).wait_send()
-            for h in range(parts):
-                there(h, k, me).wait_send()
+    def sent(owners):
+        settle(c_message.at[pl.ds(0, owners)], 0)
+        for h in range(parts):
+            settle(message.at[h, pl.ds(0, owners)], 2 + h)
 
     @pl.when(is_owner)
     def _():
+        sent(lev - 1)
         for h in range(parts):
-            for step in range(1, n):
-                home(h, mine, lax.rem(me + step, n)).wait_send()
+            settle(gathered.at[h, pl.ds(0, n - 1)], 2 + 2 * parts + h)
+
+    @pl.when(jnp.logical_not(is_owner))
+    def _():
+        sent(lev)
 
 
 def combine_kernel(cuts, plain, w_s, v_s, edges, out_hbm, buffer, done):
@@ -493,12 +500,7 @@
             pltpu.VMEM((parts, 8 * (n + 1), lat), f32),
             pltpu.VMEM((parts, 16 * lev, lat), f32),
             pltpu.SemaphoreType.DMA((7 + parts,)),
-            pltpu.SemaphoreType.DMA((lev,)),
-            pltpu.SemaphoreType.DMA((n,)),
-            pltpu.SemaphoreType.DMA((parts, lev)),
-            pltpu.SemaphoreType.DMA((parts, n)),
-            pltpu.SemaphoreType.DMA((parts, n)),
-            pltpu.SemaphoreType.DMA((parts, lev)),
+            pltpu.SemaphoreType.DMA((2 + 4 * parts,)),
         ],
         compiler_params=pltpu.CompilerParams(
             collective_id=0, has_side_effects=True, vmem_limit_bytes=32 << 20

time: 20.2 us -> 18.3 us (0.906)
  Pallas kernels: 20 us -> 18.2 us
    pallas_call x1, Pallas kernels: 18.3 us -> 16.4 us  [on_device(): pl.pallas_call(functools.partial(step_kernel, n, first_owner), out_shape=...]
where the time goes in v2:
time: 18.3 us; the launch traced here: 18.2 us
  Pallas kernels  18.2 us (99%)
    pallas_call x1, Pallas kernels, on_device(): pl.pallas_call(functools.partial(step_kernel, n, first_owner), out_shape=...  16.4 us
    pallas_call x1, Pallas kernels, on_device(): pl.pallas_call(functools.partial(combine_kernel, cuts), out_shape=jax.Sha...  1.74 us

profile of v2, /device:TPU:0, one launch (start us, length us, event | category | flops | bytes accessed | tf_op | source)
XLA Modules:
  0.0 18.2 jit_solution(2317780084697637374)
XLA Ops:
  0.0 16.4 %transport_step.1 = (f32[45,16,8,128]{3,2,1,0:T(8,128)S(1)}, f32[45,8,128]{2,1,0:T(8,128)S(1)}, f32[45,8,128]{2,1,0:T(8,128)S(1)}, f32[2,16,8,128]{3,2,1,0:T(8,128)S(1)}) custom-call(s32[8]{0:T(128)} %levels_hbm.1, s32[16]{0:T(128)} %groups_hbm.1, f32[45,16,8,128]{3,2,1,0:T(8,128)} %tracers_hbm.1, f32[45,32,128]{2,1,0:T(8,128)} %bitcast.4, ...), custom_call_target="tpu_custom_call" | custom-call | tf_op jit(solution)/shard_map/transport_step/pallas_call | solution.py:469
  16.4 1.7 %combine.1 = f32[45,16,8,128]{3,2,1,0:T(8,128)} custom-call(f32[45,16,8,128]{3,2,1,0:T(8,128)S(1)} %get-tuple-element.9.plain, f32[45,8,128]{2,1,0:T(8,128)S(1)} %get-tuple-element.10.w_s, f32[45,8,128]{2,1,0:T(8,128)S(1)} %get-tuple-element.11.v_s, f32[2,16,8,128]{3,2,1,0:T(8,128)S(1)} %get-tuple-element.12.edges), custom_call_target="tpu_custom_call" | custom-call | tf_op jit(solution)/shard_map/combine/pallas_call | solution.py:512

commit v3 on v2

--- a/solution.py
+++ b/solution.py
@@ -321,23 +321,18 @@
     def settle(block, at):
         pltpu.make_async_copy(block, block, wave.at[at]).wait()
 
+    @pl.when(is_owner)
+    def _():
+        pl.semaphore_wait(barrier, n - 1)
+
+    @pl.when(jnp.logical_not(is_owner))
+    def _():
+        pl.semaphore_wait(barrier, lev)
+
+    send(lambda k: early(k, me))
     for h in range(parts):
         sweep(h)
-        if h == 0:
-
-            @pl.when(is_owner)
-            def _():
-                pl.semaphore_wait(barrier, n - 1)
-
-            @pl.when(jnp.logical_not(is_owner))
-            def _():
-                pl.semaphore_wait(barrier, lev)
-
-            send(lambda k: early(k, me))
-            for g in range(h):
-                send(lambda k: there(g, k, me))
-        if h >= 0:
-            send(lambda k: there(h, k, me))
+        send(lambda k: there(h, k, me))
 
     @pl.when(is_owner)
     def _():

time: 18.3 us -> 17.5 us (0.956)
  Pallas kernels: 18.2 us -> 17.4 us
    pallas_call x1, Pallas kernels: 16.4 us -> 15.6 us  [on_device(): pl.pallas_call(functools.partial(step_kernel, n, first_owner), out_shape=...]
where the time goes in v3:
time: 17.5 us; the launch traced here: 17.4 us
  Pallas kernels  17.4 us (99%)
    pallas_call x1, Pallas kernels, on_device(): pl.pallas_call(functools.partial(step_kernel, n, first_owner), out_shape=...  15.6 us
    pallas_call x1, Pallas kernels, on_device(): pl.pallas_call(functools.partial(combine_kernel, cuts), out_shape=jax.Sha...  1.74 us

profile of v3, /device:TPU:0, one launch (start us, length us, event | category | flops | bytes accessed | tf_op | source)
XLA Modules:
  0.0 17.4 jit_solution(10208856321944976819)
XLA Ops:
  0.0 15.6 %transport_step.1 = (f32[45,16,8,128]{3,2,1,0:T(8,128)S(1)}, f32[45,8,128]{2,1,0:T(8,128)S(1)}, f32[45,8,128]{2,1,0:T(8,128)S(1)}, f32[2,16,8,128]{3,2,1,0:T(8,128)S(1)}) custom-call(s32[8]{0:T(128)} %levels_hbm.1, s32[16]{0:T(128)} %groups_hbm.1, f32[45,16,8,128]{3,2,1,0:T(8,128)} %tracers_hbm.1, f32[45,32,128]{2,1,0:T(8,128)} %bitcast.4, ...), custom_call_target="tpu_custom_call" | custom-call | tf_op jit(solution)/shard_map/transport_step/pallas_call | solution.py:464
  15.6 1.7 %combine.1 = f32[45,16,8,128]{3,2,1,0:T(8,128)} custom-call(f32[45,16,8,128]{3,2,1,0:T(8,128)S(1)} %get-tuple-element.9.plain, f32[45,8,128]{2,1,0:T(8,128)S(1)} %get-tuple-element.10.w_s, f32[45,8,128]{2,1,0:T(8,128)S(1)} %get-tuple-element.11.v_s, f32[2,16,8,128]{3,2,1,0:T(8,128)S(1)} %get-tuple-element.12.edges), custom_call_target="tpu_custom_call" | custom-call | tf_op jit(solution)/shard_map/combine/pallas_call | solution.py:507

commit v4 on v3

--- a/solution.py
+++ b/solution.py
@@ -52,22 +52,29 @@
 
 
 def solve_level(n, h, back_s, gathered, solved):
+    top, low = pl.ds(0, 4), pl.ds(4, 4)
+
+    def factor(c, d):
+        return back_s[c, d, top, :]
+
     y_prev = 0.0
     ys = []
     for d in range(n):
         e = (d + 1) % n
-        right = gathered[h, d, pl.ds(0, 8), :] - back_s[0, d] * gathered[h, e, pl.ds(8, 8), :]
+        right = gathered[h, d, top, :] - factor(0, d) * gathered[h, e, low, :]
         if d < n - 1:
-            y_prev = right * back_s[2, d] - back_s[1, d] * y_prev
+            y_prev = right * factor(2, d) - factor(1, d) * y_prev
             ys.append(y_prev)
     for d in range(n - 3, -1, -1):
-        ys[d] = ys[d] - back_s[3, d] * ys[d + 1]
+        ys[d] = ys[d] - factor(3, d) * ys[d + 1]
     end = n - 1
-    x_end = (right - back_s[1, end] * ys[end - 1] - back_s[3, end] * ys[0]) * back_s[2, end]
-    solved[h, pl.ds(0, 8), :] = x_end
-    solved[h, pl.ds(8 * n, 8), :] = x_end
+    x_end = (right - factor(1, end) * ys[end - 1] - factor(3, end) * ys[0]) * factor(2, end)
+    solved[h, 0, top, :] = x_end
+    solved[h, end, low, :] = x_end
     for d in range(n - 1):
-        solved[h, pl.ds(8 * (d + 1), 8), :] = ys[d] + back_s[4, d] * x_end
+        value = ys[d] + factor(4, d) * x_end
+        solved[h, d, low, :] = value
+        solved[h, d + 1, top, :] = value
 
 
 def step_kernel(
@@ -116,6 +123,7 @@
     cells, count, lev, lat = tracers.shape
     kinds = emissions.shape[1]
     parts = count // 8
+    waves = count // 4
     last = cells - 1
     me = lax.axis_index("lon")
     ens = lax.axis_index("ens")
@@ -177,17 +185,17 @@
         return remote(
             message.at[h, k],
             gathered.at[h, sender],
-            wave.at[2 + h],
-            wave.at[2 + parts + h],
+            wave.at[3],
+            wave.at[4 + h],
             first_owner + k,
         )
 
     def home(h, k, device):
         return remote(
-            solved.at[h, pl.ds(8 * device, 16), :],
-            back.at[h, pl.ds(16 * k, 16), :],
-            wave.at[2 + 2 * parts + h],
-            wave.at[2 + 3 * parts + h],
+            solved.at[h, device],
+            back.at[h, pl.ds(8 * k, 8), :],
+            wave.at[2],
+            wave.at[4 + waves + h],
             device,
         )
 
@@ -267,7 +275,7 @@
         c_message[k] = c_s[pl.ds(k, 8, stride=8), :]
 
     def shifted(i, h):
-        values = [tracers[i, 8 * h + t] for t in range(8)]
+        values = [tracers[i, 4 * h + t] for t in range(4)]
         return (
             tuple(pltpu.roll(value, 1, 1) for value in values),
             tuple(pltpu.roll(value, lat - 1, 1) for value in values),
@@ -277,9 +285,9 @@
         south, here, after = south_s[i], here_s[i], after_s[i]
         return [
             south * souths[t]
-            + here * tracers[i, 8 * h + t]
-            + (source_s[i * kinds + group[8 * h + t]] - after * norths[t])
-            for t in range(8)
+            + here * tracers[i, 4 * h + t]
+            + (source_s[i * kinds + group[4 * h + t]] - after * norths[t])
+            for t in range(4)
         ]
 
     def forward(h, i, carry):
@@ -288,14 +296,15 @@
         values, firsts = [], []
         for t, right in enumerate(rights(h, i, souths, norths)):
             value = right - low * before[t]
-            plain[i, 8 * h + t] = value
+            plain[i, 4 * h + t] = value
             values.append(value)
             firsts.append(sums[t] + weight * value)
         return (tuple(values), tuple(firsts), *shifted(i + 1, h))
 
     def sweep(h):
-        copies[7 + h].wait()
-        nothing = (zeros,) * 8
+        if h % 2 == 0:
+            copies[7 + h // 2].wait()
+        nothing = (zeros,) * 4
         ends, firsts, souths, norths = lax.fori_loop(
             0, last, functools.partial(forward, h), (nothing, nothing, *shifted(0, h)), unroll=22
         )
@@ -303,15 +312,15 @@
             p_s[pl.ds(t * lev, lev), :] = right - lower_last * ends[t]
             q_s[pl.ds(t * lev, lev), :] = firsts[t]
         for k in range(lev):
-            rows = pl.ds(k, 8, stride=lev)
-            message[h, k, pl.ds(0, 8), :] = p_s[rows, :]
-            message[h, k, pl.ds(8, 8), :] = q_s[rows, :]
+            rows = pl.ds(k, 4, stride=lev)
+            message[h, k, pl.ds(0, 4), :] = p_s[rows, :]
+            message[h, k, pl.ds(4, 4), :] = q_s[rows, :]
 
     def send(copy_of):
         @pl.when(is_owner)
         def _():
             for step in range(1, lev):
-                copy_of(lax.rem(mine + step, lev)).start()
+                copy_of(step - 1 + jnp.where(step - 1 < mine, 0, 1)).start()
 
         @pl.when(jnp.logical_not(is_owner))
         def _():
@@ -330,14 +339,14 @@
         pl.semaphore_wait(barrier, lev)
 
     send(lambda k: early(k, me))
-    for h in range(parts):
+    for h in range(waves):
         sweep(h)
         send(lambda k: there(h, k, me))
 
     @pl.when(is_owner)
     def _():
         coefs[me] = c_message[mine]
-        for h in range(parts):
+        for h in range(waves):
             gathered[h, me] = message[h, mine]
 
     def spikes(step, carry):
@@ -373,17 +382,17 @@
         others = pl.ds(0, n - 1)
         settle(coefs.at[others], 1)
         factor_levels(n, kappa, coefs, back_s)
-        for h in range(parts):
-            settle(gathered.at[h, others], 2 + parts + h)
+        for h in range(waves):
+            settle(gathered.at[h, others], 4 + h)
             solve_level(n, h, back_s, gathered, solved)
             for step in range(n - 1):
                 home(h, mine, step + jnp.where(step < me, 0, 1)).start()
-            back[h, pl.ds(16 * mine, 16), :] = solved[h, pl.ds(8 * me, 16), :]
+            back[h, pl.ds(8 * mine, 8), :] = solved[h, me]
 
     def finish(h, owners):
-        settle(back.at[h, pl.ds(0, 16 * owners)], 2 + 3 * parts + h)
-
-    for h in range(parts):
+        settle(back.at[h, pl.ds(0, 8 * owners)], 4 + waves + h)
+
+    for h in range(waves):
 
         @pl.when(is_owner)
         def _():
@@ -394,19 +403,17 @@
             finish(h, lev)
 
         for j in range(2):
-            for t in range(8):
-                out[j, h * 8 + t] = back[h, pl.ds(j * 8 + t, lev, stride=16), :]
+            for t in range(4):
+                out[j, h * 4 + t] = back[h, pl.ds(j * 4 + t, lev, stride=8), :]
 
     def sent(owners):
         settle(c_message.at[pl.ds(0, owners)], 0)
-        for h in range(parts):
-            settle(message.at[h, pl.ds(0, owners)], 2 + h)
+        settle(message.at[:, pl.ds(0, owners)], 3)
 
     @pl.when(is_owner)
     def _():
         sent(lev - 1)
-        for h in range(parts):
-            settle(gathered.at[h, pl.ds(0, n - 1)], 2 + 2 * parts + h)
+        settle(gathered.at[:, pl.ds(0, n - 1)], 2)
 
     @pl.when(jnp.logical_not(is_owner))
     def _():
@@ -437,7 +444,7 @@
 def on_device(tracers, zonal_flux, merid_flux, kappa, levels, groups, emissions, limiter):
     n = lax.axis_size("lon")
     cells, count, lev, lat = tracers.shape
-    parts, kinds = count // 8, emissions.shape[0]
+    parts, waves, kinds = count // 8, count // 4, emissions.shape[0]
     first_owner = (n - lev) // 2
     assert lev == 8 and count % 8 == 0 and n >= lev
     f32 = jnp.float32
@@ -488,14 +495,14 @@
             pltpu.VMEM((8 * lev, lat), f32),
             pltpu.VMEM((64, lat), f32),
             pltpu.VMEM((lev, 8, lat), f32),
-            pltpu.VMEM((parts, lev, 16, lat), f32),
+            pltpu.VMEM((waves, lev, 8, lat), f32),
             pltpu.VMEM((n, 8, lat), f32),
-            pltpu.VMEM((parts, n, 16, lat), f32),
+            pltpu.VMEM((waves, n, 8, lat), f32),
             pltpu.VMEM((5, n, 8, lat), f32),
-            pltpu.VMEM((parts, 8 * (n + 1), lat), f32),
-            pltpu.VMEM((parts, 16 * lev, lat), f32),
+            pltpu.VMEM((waves, n, 8, lat), f32),
+            pltpu.VMEM((waves, 8 * lev, lat), f32),
             pltpu.SemaphoreType.DMA((7 + parts,)),
-            pltpu.SemaphoreType.DMA((2 + 4 * parts,)),
+            pltpu.SemaphoreType.DMA((4 + 2 * waves,)),
         ],
         compiler_params=pltpu.CompilerParams(
             collective_id=0, has_side_effects=True, vmem_limit_bytes=32 << 20

time: 17.5 us -> 17.5 us (level)
  no operation moved by 1% of the time
where the time goes in v4:
time: 17.5 us; the launch traced here: 17.3 us
  Pallas kernels  17.3 us (99%)
    pallas_call x1, Pallas kernels, on_device(): pl.pallas_call(functools.partial(step_kernel, n, first_owner), out_shape=...  15.6 us
    pallas_call x1, Pallas kernels, on_device(): pl.pallas_call(functools.partial(combine_kernel, cuts), out_shape=jax.Sha...  1.74 us

profile of v4, /device:TPU:0, one launch (start us, length us, event | category | flops | bytes accessed | tf_op | source)
XLA Modules:
  0.0 17.3 jit_solution(7774012843086140251)
XLA Ops:
  0.0 15.6 %transport_step.1 = (f32[45,16,8,128]{3,2,1,0:T(8,128)S(1)}, f32[45,8,128]{2,1,0:T(8,128)S(1)}, f32[45,8,128]{2,1,0:T(8,128)S(1)}, f32[2,16,8,128]{3,2,1,0:T(8,128)S(1)}) custom-call(s32[8]{0:T(128)} %levels_hbm.1, s32[16]{0:T(128)} %groups_hbm.1, f32[45,16,8,128]{3,2,1,0:T(8,128)} %tracers_hbm.1, f32[45,32,128]{2,1,0:T(8,128)} %bitcast.4, ...), custom_call_target="tpu_custom_call" | custom-call | tf_op jit(solution)/shard_map/transport_step/pallas_call | solution.py:471
  15.6 1.7 %combine.1 = f32[45,16,8,128]{3,2,1,0:T(8,128)} custom-call(f32[45,16,8,128]{3,2,1,0:T(8,128)S(1)} %get-tuple-element.9.plain, f32[45,8,128]{2,1,0:T(8,128)S(1)} %get-tuple-element.10.w_s, f32[45,8,128]{2,1,0:T(8,128)S(1)} %get-tuple-element.11.v_s, f32[2,16,8,128]{3,2,1,0:T(8,128)S(1)} %get-tuple-element.12.edges), custom_call_target="tpu_custom_call" | custom-call | tf_op jit(solution)/shard_map/combine/pallas_call | solution.py:514

commit v5 on v4

--- a/solution.py
+++ b/solution.py
@@ -124,6 +124,7 @@
     kinds = emissions.shape[1]
     parts = count // 8
     waves = count // 4
+    prompt = min(4, first_owner)
     last = cells - 1
     me = lax.axis_index("lon")
     ens = lax.axis_index("ens")
@@ -158,11 +159,6 @@
         for step in range(1, n):
             greet(lax.rem(me + step, n))
 
-    @pl.when(jnp.logical_not(is_owner))
-    def _():
-        for k in range(lev):
-            greet(first_owner + k)
-
     for copy in copies[4:]:
         copy.start()
 
@@ -196,6 +192,15 @@
             back.at[h, pl.ds(8 * k, 8), :],
             wave.at[2],
             wave.at[4 + waves + h],
+            device,
+        )
+
+    def rest(k, device):
+        return remote(
+            solved.at[:, device],
+            back.at[:, pl.ds(8 * k, 8), :],
+            wave.at[2],
+            wave.at[4 + waves],
             device,
         )
 
@@ -332,7 +337,7 @@
 
     @pl.when(is_owner)
     def _():
-        pl.semaphore_wait(barrier, n - 1)
+        pl.semaphore_wait(barrier, lev - 1)
 
     @pl.when(jnp.logical_not(is_owner))
     def _():
@@ -385,23 +390,23 @@
         for h in range(waves):
             settle(gathered.at[h, others], 4 + h)
             solve_level(n, h, back_s, gathered, solved)
-            for step in range(n - 1):
-                home(h, mine, step + jnp.where(step < me, 0, 1)).start()
+            for device in range(prompt):
+                home(h, mine, device).start()
             back[h, pl.ds(8 * mine, 8), :] = solved[h, me]
-
-    def finish(h, owners):
-        settle(back.at[h, pl.ds(0, 8 * owners)], 4 + waves + h)
+        for step in range(prompt, n - 1):
+            rest(mine, step + jnp.where(step < me, 0, 1)).start()
+        settle(back.at[:, pl.ds(0, 8 * (lev - 1))], 4 + waves)
+
+    @pl.when(me < prompt)
+    def _():
+        for h in range(waves):
+            settle(back.at[h, pl.ds(0, 8 * lev)], 4 + waves + h)
+
+    @pl.when(jnp.logical_and(me >= prompt, jnp.logical_not(is_owner)))
+    def _():
+        settle(back.at[:, pl.ds(0, 8 * lev)], 4 + waves)
 
     for h in range(waves):
-
-        @pl.when(is_owner)
-        def _():
-            finish(h, lev - 1)
-
-        @pl.when(jnp.logical_not(is_owner))
-        def _():
-            finish(h, lev)
-
         for j in range(2):
             for t in range(4):
                 out[j, h * 4 + t] = back[h, pl.ds(j * 4 + t, lev, stride=8), :]

time: 17.5 us -> 17.2 us (0.983)
  Pallas kernels: 17.3 us -> 17.1 us
    pallas_call x1, Pallas kernels: 15.6 us -> 15.3 us  [on_device(): pl.pallas_call(functools.partial(step_kernel, n, first_owner), out_shape=...]
where the time goes in v5:
time: 17.2 us; the launch traced here: 17.1 us
  Pallas kernels  17.1 us (99%)
    pallas_call x1, Pallas kernels, on_device(): pl.pallas_call(functools.partial(step_kernel, n, first_owner), out_shape=...  15.3 us
    pallas_call x1, Pallas kernels, on_device(): pl.pallas_call(functools.partial(combine_kernel, cuts), out_shape=jax.Sha...  1.74 us

profile of v5, /device:TPU:0, one launch (start us, length us, event | category | flops | bytes accessed | tf_op | source)
XLA Modules:
  0.0 17.1 jit_solution(18163701498360898908)
XLA Ops:
  0.0 15.3 %transport_step.1 = (f32[45,16,8,128]{3,2,1,0:T(8,128)S(1)}, f32[45,8,128]{2,1,0:T(8,128)S(1)}, f32[45,8,128]{2,1,0:T(8,128)S(1)}, f32[2,16,8,128]{3,2,1,0:T(8,128)S(1)}) custom-call(s32[8]{0:T(128)} %levels_hbm.1, s32[16]{0:T(128)} %groups_hbm.1, f32[45,16,8,128]{3,2,1,0:T(8,128)} %tracers_hbm.1, f32[45,32,128]{2,1,0:T(8,128)} %bitcast.4, ...), custom_call_target="tpu_custom_call" | custom-call | tf_op jit(solution)/shard_map/transport_step/pallas_call | solution.py:476
  15.4 1.7 %combine.1 = f32[45,16,8,128]{3,2,1,0:T(8,128)} custom-call(f32[45,16,8,128]{3,2,1,0:T(8,128)S(1)} %get-tuple-element.9.plain, f32[45,8,128]{2,1,0:T(8,128)S(1)} %get-tuple-element.10.w_s, f32[45,8,128]{2,1,0:T(8,128)S(1)} %get-tuple-element.11.v_s, f32[2,16,8,128]{3,2,1,0:T(8,128)S(1)} %get-tuple-element.12.edges), custom_call_target="tpu_custom_call" | custom-call | tf_op jit(solution)/shard_map/combine/pallas_call | solution.py:519

commit v6 on v5

--- a/solution.py
+++ b/solution.py
@@ -174,7 +174,7 @@
 
     def early(k, sender):
         return remote(
-            c_message.at[k], coefs.at[sender], wave.at[0], wave.at[1], first_owner + k
+            c_message.at[k, pl.ds(0, 5)], coefs.at[sender, pl.ds(0, 5)], wave.at[0], wave.at[1], first_owner + k
         )
 
     def there(h, k, sender):
@@ -385,7 +385,7 @@
     @pl.when(is_owner)
     def _():
         others = pl.ds(0, n - 1)
-        settle(coefs.at[others], 1)
+        settle(coefs.at[others, pl.ds(0, 5)], 1)
         factor_levels(n, kappa, coefs, back_s)
         for h in range(waves):
             settle(gathered.at[h, others], 4 + h)
@@ -412,7 +412,7 @@
                 out[j, h * 4 + t] = back[h, pl.ds(j * 4 + t, lev, stride=8), :]
 
     def sent(owners):
-        settle(c_message.at[pl.ds(0, owners)], 0)
+        settle(c_message.at[pl.ds(0, owners), pl.ds(0, 5)], 0)
         settle(message.at[:, pl.ds(0, owners)], 3)
 
     @pl.when(is_owner)

time: 17.2 us -> 17.2 us (level)
  no operation moved by 1% of the time
where the time goes in v6:
time: 17.2 us; the launch traced here: 17 us
  Pallas kernels  17 us (99%)
    pallas_call x1, Pallas kernels, on_device(): pl.pallas_call(functools.partial(step_kernel, n, first_owner), out_shape=...  15.3 us
    pallas_call x1, Pallas kernels, on_device(): pl.pallas_call(functools.partial(combine_kernel, cuts), out_shape=jax.Sha...  1.74 us

profile of v6, /device:TPU:0, one launch (start us, length us, event | category | flops | bytes accessed | tf_op | source)
XLA Modules:
  0.0 17.0 jit_solution(17502855741670102122)
XLA Ops:
  0.0 15.3 %transport_step.1 = (f32[45,16,8,128]{3,2,1,0:T(8,128)S(1)}, f32[45,8,128]{2,1,0:T(8,128)S(1)}, f32[45,8,128]{2,1,0:T(8,128)S(1)}, f32[2,16,8,128]{3,2,1,0:T(8,128)S(1)}) custom-call(s32[8]{0:T(128)} %levels_hbm.1, s32[16]{0:T(128)} %groups_hbm.1, f32[45,16,8,128]{3,2,1,0:T(8,128)} %tracers_hbm.1, f32[45,32,128]{2,1,0:T(8,128)} %bitcast.4, ...), custom_call_target="tpu_custom_call" | custom-call | tf_op jit(solution)/shard_map/transport_step/pallas_call | solution.py:476
  15.3 1.7 %combine.1 = f32[45,16,8,128]{3,2,1,0:T(8,128)} custom-call(f32[45,16,8,128]{3,2,1,0:T(8,128)S(1)} %get-tuple-element.9.plain, f32[45,8,128]{2,1,0:T(8,128)S(1)} %get-tuple-element.10.w_s, f32[45,8,128]{2,1,0:T(8,128)S(1)} %get-tuple-element.11.v_s, f32[2,16,8,128]{3,2,1,0:T(8,128)S(1)} %get-tuple-element.12.edges), custom_call_target="tpu_custom_call" | custom-call | tf_op jit(solution)/shard_map/combine/pallas_call | solution.py:519
